TPU v7x, 256 devices: a whole 4x4x8 slice. The times are simulated.
256 devices in a mesh: head: 16 (over x, y), key: 8 (over z), row: 2 (over core).
Axes of the slice: x: 4, y: 4, z: 8, core: 2. Of those that a mesh axis runs over, the one named last changes fastest.
Arguments:
- mla_query: bfloat16 [256, 128, 576], P('row', 'head'), may hold values from -48 to 48
- mla_cache: bfloat16 [16, 2048, 576], P(None, 'key'), may hold values from -6 to 6
- index_query: bfloat16 [256, 64, 128], P('row'), may hold values from -24 to 24
- index_keys: bfloat16 [32768, 128], P(('head', 'key')), may hold values from -6 to 6
- index_weight: float32 [256, 64], P('row'), may hold values from -0.75 to 0.75
Outputs:
- query_grad: float32 [256, 64, 128], P('row', 'head')
- key_grad: float32 [32768, 128], P(('head', 'key', 'row'))
- weight_grad: float32 [256, 64], P('row')
All inputs are finite; a program needn't handle non-finite values.
Results may differ from a plain program's by a relative error of at most 0.0029.
Values sent between devices are 32-bit elements; how exact they have to be, the bound alone decides.
No kernel may reach another device: no remote copies, remote signals or barrier semaphores. Data moves between devices by JAX's collectives and lax.ppermute only.
A program may use at most 128 MiB of HBM per device.

v0:
```python
import math
import jax
import jax.numpy as jnp
from jax import lax
from jax.sharding import PartitionSpec as P

MH = 128


def shards(mla_query, mla_cache, index_query, index_keys, index_weight):
    key_count = lax.axis_size("key")
    head_count = lax.axis_size("head")
    block_count = mla_cache.shape[0]
    local_keys = mla_cache.shape[1]
    row_local = mla_query.shape[0]
    cache_rows = mla_cache.reshape(block_count * local_keys, mla_cache.shape[2])
    scores = jnp.einsum(
        "thd,sd->ths", mla_query, cache_rows, preferred_element_type=jnp.float32
    ) * (1.0 / math.sqrt(192.0))
    top_score = lax.pmax(jnp.max(scores, axis=2), "key")
    exp_terms = jnp.exp(scores - top_score[:, :, None])
    sum_terms = lax.psum(jnp.sum(exp_terms, axis=2), "key")
    head_scale = 1.0 / sum_terms
    partial_value = jnp.sum(exp_terms * head_scale[:, :, None], axis=1) / MH
    spread = partial_value.reshape(row_local, block_count, local_keys)
    summed_all = lax.psum(spread, "head")
    target = lax.dynamic_slice_in_dim(summed_all, lax.axis_index("head"), 1, 1).reshape(
        row_local, local_keys
    )
    root_width = math.sqrt(index_keys.shape[1])
    products = jnp.einsum(
        "thd,sd->ths", index_query, index_keys, preferred_element_type=jnp.float32
    )
    active = jnp.maximum(products, 0.0)
    logits = jnp.sum(active * index_weight[:, :, None], axis=1) / root_width
    top_logit = lax.pmax(jnp.max(logits, axis=1), ("head", "key"))
    exp_logit = jnp.exp(logits - top_logit[:, None])
    logit_sum = lax.psum(jnp.sum(exp_logit, axis=1), ("head", "key"))
    soft_probs = exp_logit / logit_sum[:, None]
    key_total = index_keys.shape[0] * head_count * key_count
    dlogits = key_total * (soft_probs - target)
    weight_part = jnp.sum(active * dlogits[:, None, :], axis=2) / root_width
    slope_terms = (
        dlogits[:, None, :]
        * index_weight[:, :, None]
        * jnp.where(products > 0.0, 1.0, 0.0)
        / root_width
    ).astype(jnp.bfloat16)
    query_part = jnp.einsum(
        "ths,sd->thd", slope_terms, index_keys, preferred_element_type=jnp.float32
    )
    keys_part = jnp.einsum(
        "ths,thd->sd", slope_terms, index_query, preferred_element_type=jnp.float32
    )
    key_grad = lax.psum_scatter(keys_part, "row", scatter_dimension=0, tiled=True)
    head_share = query_part.shape[1] // head_count
    query_full, weight_grad = lax.psum((query_part, weight_part), ("head", "key"))
    query_grad = lax.dynamic_slice_in_dim(
        query_full, lax.axis_index("head") * head_share, head_share, 1
    )
    return (query_grad, key_grad, weight_grad)


def solution(mesh):
    placed = (
        P("row", "head", None),
        P(None, "key", None),
        P("row", None, None),
        P(("head", "key"), None),
        P("row", None),
    )
    return jax.shard_map(
        shards,
        mesh=mesh,
        in_specs=placed,
        out_specs=(P("row", "head", None), P(("head", "key", "row"), None), P("row", None)),
        check_vma=False,
    )
```

profile of v0, /device:TPU:0, one launch (start us, length us, event | category | flops | bytes accessed | tf_op | source)
XLA Modules:
  0.0 1499.3 jit_solution(123140552502343702)
XLA Ops:
  7.2 0.0 copy-start
  7.2 0.0 all-reduce.3.cloned.1.call-start
  7.2 7.2 copy.19
  14.4 8.3 reshape.73
  22.7 0.0 copy-done
  22.7 12.6 multiply_reduce_fusion.1
  35.3 18.2 %pmax.15 = f32[128,8]{0,1:T(8,128)S(1)} all-reduce(f32[128,8]{0,1:T(8,128)S(1)} %get-tuple-element.12), channel_id=1, replica_groups=mesh['head'=16,'key'=8,'row'=2] {'key'}, use_global_device_ids=true, to_apply=%region_6.0 | all-reduce | flops 1024 | bytes 8192 | tf_op jit(solution)/shard_map/pmax | solution.py:20
  53.6 8.6 fusion
  62.2 14.2 psum.36
  76.4 8.0 multiply_reduce_fusion
  84.4 0.0 copy-start.2
  84.4 0.0 copy-start.3
  84.4 0.2 broadcast_multiply_fusion
  84.6 1.9 copy.20
  86.4 3.0 copy.21
  89.4 0.0 all-reduce.3.cloned.1.call-update
  89.4 0.2 all-reduce.5.cloned.1.call-start
  89.7 0.0 copy-done.2
  89.7 0.0 copy-done.3
  89.7 6.8 multiply_reduce_fusion.3
  96.4 0.1 multiply_reduce_fusion.4
  96.5 349.1 %pmax.14 = f32[128]{0:T(128)S(1)} all-reduce(f32[128]{0:T(128)S(1)} %multiply_reduce_fusion.4), channel_id=1, replica_groups=mesh['head'=16,'key'=8,'row'=2] {'head','key'}, use_global_device_ids=true, to_apply=%region_2.0 | all-reduce | flops 128 | bytes 1024 | tf_op jit(solution)/shard_map/pmax | solution.py:36
  445.7 0.2 exponential_reduce_fusion
  445.9 342.2 %psum.35 = f32[128]{0:T(128)S(1)} all-reduce(f32[128]{0:T(128)S(1)} %exponential_reduce_fusion), channel_id=1, replica_groups=mesh['head'=16,'key'=8,'row'=2] {'head','key'}, use_global_device_ids=true, to_apply=%region_4.0 | all-reduce | flops 128 | bytes 1024 | tf_op jit(solution)/shard_map/psum | solution.py:38
  788.0 0.0 all-reduce.3.cloned.1.call-done
  788.0 1.0 fusion.12
  789.1 5.7 fusion.13
  794.8 0.0 copy-start.1
  794.8 0.0 all-reduce.5.cloned.1.call-update
  794.8 0.0 reduce-scatter.2.cloned.1.call-start
  794.9 4.7 multiply_reduce_fusion.2
  799.6 0.0 copy-done.1
  799.6 7.0 fusion.5
  806.6 0.0 reduce-scatter.2.cloned.1.call-update
  806.6 684.3 %psum.39 = f32[128,64]{0,1:T(8,128)} all-reduce(f32[128,64]{0,1:T(8,128)S(1)} %broadcast_multiply_fusion.1), channel_id=1, replica_groups=mesh['head'=16,'key'=8,'row'=2] {'head','key'}, use_global_device_ids=true, to_apply=%region_14.15 | all-reduce | flops 8192 | bytes 65536 | tf_op jit(solution)/shard_map/psum | solution.py:57
  1490.9 0.0 all-reduce.5.cloned.1.call-done
  1490.9 1.0 constant_dynamic-slice_fusion
  1491.9 0.9 copy.24
  1492.8 0.0 reduce-scatter.2.cloned.1.call-done
  (2 shorter events, 0.0 us)
Async XLA Ops:
  7.2 15.6 %copy-start = (bf16[128,8,576]{0,2,1:T(8,128)(2,1)S(1)}, bf16[128,8,576]{0,2,1:T(8,128)(2,1)}, u32[]{:S(2)}) copy-start(bf16[128,8,576]{0,2,1:T(8,128)(2,1)} %param.5) | copy-start | bytes 3538948
  7.2 780.8 %all-reduce.3.cloned.1.call-start = ((), (), s32[]{:S(2)}) async-start(), calls=%async_computation.1 | async-start | bytes 4194304 | tf_op jit(solution)/shard_map/psum | solution.py:26
  84.4 5.3 copy-start.2
  84.4 5.3 copy-start.3
  89.4 1401.5 %all-reduce.5.cloned.1.call-start = ((), (), s32[]{:S(2)}) async-start(), calls=%async_computation.2 | async-start | bytes 8388608 | tf_op jit(solution)/shard_map/psum | solution.py:57
  794.8 4.8 copy-start.1
  794.8 697.9 %reduce-scatter.2.cloned.1.call-start = ((), (), s32[]{:S(2)}) async-start(), calls=%async_computation.3 | async-start | bytes 196608 | tf_op jit(solution)/shard_map/reduce_scatter | solution.py:55
Sparse Core Ops, SparseCore 0:
  89.5 99.6 all-reduce.2
  795.0 227.7 all-reduce.4
  1025.8 10.1 reduce-scatter.1
where the time goes:
time: 1500 us
  blocking collectives  1410 us (94%)
  matrix products  32.1 us (2%)
  other arithmetic  22.8 us (2%)
  local copies, waits for them, and re-layouts  22.2 us (1%)
    psum x1, blocking collectives, shards(): lax.psum((query_part, weight_part), ('head', 'key'))  684 us
    pmax x1, blocking collectives, shards(): top_logit = lax.pmax(jnp.max(logits, axis=1), ('head', 'key'))  349 us
    psum x1, blocking collectives, shards(): logit_sum = lax.psum(jnp.sum(exp_logit, axis=1), ('head', 'key'))  342 us
  transfers between devices with their start and end apart: 3, of which 0 were waited for; matrix products, arithmetic and copies ran while one was open for 1% of the time, Pallas kernels for 0%

commit v1 on v0

--- a/solution.py
+++ b/solution.py
@@ -35,7 +35,7 @@
     logits = jnp.sum(active * index_weight[:, :, None], axis=1) / root_width
     top_logit = lax.pmax(jnp.max(logits, axis=1), ("head", "key"))
     exp_logit = jnp.exp(logits - top_logit[:, None])
-    logit_sum = lax.psum(jnp.sum(exp_logit, axis=1), ("head", "key"))
+    logit_sum = lax.psum(lax.psum(jnp.sum(exp_logit, axis=1), "key"), "head")
     soft_probs = exp_logit / logit_sum[:, None]
     key_total = index_keys.shape[0] * head_count * key_count
     dlogits = key_total * (soft_probs - target)

time: 1500 us -> 1250 us (0.83)
  blocking collectives: 1410 us -> 1100 us
  waiting for transfers between devices: 0.05 us -> 57.4 us
    psum x1, blocking collectives: 342 us -> 35.9 us  [shards(): logit_sum = lax.psum(lax.psum(jnp.sum(exp_logit, axis=1), 'key'), 'head')]
    psum x1, waiting for transfers between devices: 0.01 us -> 57.3 us  [shards(): summed_all = lax.psum(spread, 'head')]
  transfers between devices with their start and end apart: 3 -> 3, of which waited for: 0 -> 1; matrix products, arithmetic and copies ran while one was open for 1% -> 1% of each run, Pallas kernels for 0% -> 0%
where the time goes in v1:
time: 1250 us
  blocking collectives  1100 us (88%)
  waiting for transfers between devices  57.4 us (5%)
  matrix products  32.4 us (3%)
  other arithmetic  22.8 us (2%)
  local copies, waits for them, and re-layouts  22.1 us (2%)
  between operations  13.9 us (1%)
    psum x1, blocking collectives, shards(): lax.psum((query_part, weight_part), ('head', 'key'))  688 us
    pmax x1, blocking collectives, shards(): top_logit = lax.pmax(jnp.max(logits, axis=1), ('head', 'key'))  347 us
    psum x1, waiting for transfers between devices, shards(): summed_all = lax.psum(spread, 'head')  57.3 us
    psum x1, blocking collectives, shards(): logit_sum = lax.psum(lax.psum(jnp.sum(exp_logit, axis=1), 'key'), 'head')  35.9 us
  transfers between devices with their start and end apart: 3, of which 1 were waited for; matrix products, arithmetic and copies ran while one was open for 1% of the time, Pallas kernels for 0%

profile of v1, /device:TPU:0, one launch (start us, length us, event | category | flops | bytes accessed | tf_op | source)
XLA Modules:
  0.0 1251.8 jit_solution(4740036782024080848)
XLA Ops:
  7.2 0.0 copy-start
  7.2 0.0 all-reduce.4.cloned.1.call-start
  7.2 7.2 copy.19
  14.4 8.3 reshape.73
  22.7 0.0 copy-done
  22.7 0.0 copy-start.1
  22.7 0.0 copy-start.3
  22.7 0.0 copy-start.4
  22.8 12.8 %multiply_reduce_fusion.1 = (f32[128,8]{0,1:T(8,128)S(1)}, f32[128,8,4096]{2,0,1:T(8,128)}) fusion(bf16[128,8,576]{0,2,1:T(8,128)(2,1)S(1)} %copy-done, bf16[4096,576,1]{0,1,2:T(8,128)(2,1)} %reshape.73), kind=kOutput, calls=%fused_computation.2 | convolution fusion | flops 4840225792 | bytes 22679552 | tf_op jit(solution)/shard_map/thd,sd->ths/dot_general | solution.py:17
  35.5 18.2 %pmax.15 = f32[128,8]{0,1:T(8,128)S(1)} all-reduce(f32[128,8]{0,1:T(8,128)S(1)} %get-tuple-element.14), channel_id=1, replica_groups=mesh['head'=16,'key'=8,'row'=2] {'key'}, use_global_device_ids=true, to_apply=%region_7.0 | all-reduce | flops 1024 | bytes 8192 | tf_op jit(solution)/shard_map/pmax | solution.py:20
  53.8 0.0 copy-done.1
  53.8 0.0 copy-done.3
  53.8 0.0 copy-done.4
  53.8 6.8 multiply_reduce_fusion.3
  60.6 0.1 multiply_reduce_fusion.4
  60.7 346.6 %pmax.14 = f32[128]{0:T(128)S(1)} all-reduce(f32[128]{0:T(128)S(1)} %multiply_reduce_fusion.4), channel_id=1, replica_groups=mesh['head'=16,'key'=8,'row'=2] {'head','key'}, use_global_device_ids=true, to_apply=%region_2.0 | all-reduce | flops 128 | bytes 1024 | tf_op jit(solution)/shard_map/pmax | solution.py:36
  407.3 0.2 exponential_reduce_fusion
  407.5 8.6 fusion
  416.1 14.6 %all-reduce = (f32[128,8]{0,1:T(8,128)S(1)}, f32[128]{0:T(128)S(1)}) all-reduce(f32[128,8]{0,1:T(8,128)S(1)} %fusion, f32[128]{0:T(128)S(1)} %exponential_reduce_fusion), channel_id=1, replica_groups=mesh['head'=16,'key'=8,'row'=2] {'key'}, use_global_device_ids=true, to_apply=%region_9.0 | all-reduce | flops 1152 | bytes 9216 | tf_op jit(solution)/shard_map/psum | solution.py:22
  430.7 8.0 multiply_reduce_fusion
  438.7 0.2 broadcast_multiply_fusion
  438.9 1.8 copy.20
  440.7 2.9 copy.21
  443.7 0.0 all-reduce.4.cloned.1.call-update
  443.7 0.0 all-reduce.6.cloned.1.call-start
  443.7 35.9 %psum.43 = f32[128]{0:T(128)S(1)} all-reduce(f32[128]{0:T(128)S(1)} %get-tuple-element.13), channel_id=1, replica_groups=mesh['head'=16,'key'=8,'row'=2] {'head'}, use_global_device_ids=true, to_apply=%region_5.0 | all-reduce | flops 128 | bytes 1024 | tf_op jit(solution)/shard_map/psum | solution.py:38
  479.6 57.3 %all-reduce.4.cloned.1.call-done = f32[128,16,256]{2,0,1:T(8,128)} async-done(((f32[128,16,256]{2,0,1:T(8,128)}), f32[128,16,256]{2,0,1:T(8,128)}) %all-reduce.4.cloned.1.call-update) | async-done | bytes 2097168 | tf_op jit(solution)/shard_map/psum | solution.py:26
  537.0 1.0 fusion.12
  538.0 5.8 fusion.13
  543.8 0.0 copy-start.2
  543.8 0.0 copy-start.5
  543.8 0.0 all-reduce.6.cloned.1.call-update
  543.8 0.0 reduce-scatter.2.cloned.1.call-start
  543.9 4.7 multiply_reduce_fusion.2
  548.5 0.0 copy-done.2
  548.6 0.0 copy-done.5
  548.6 7.0 fusion.5
  555.6 0.0 reduce-scatter.2.cloned.1.call-update
  555.6 687.8 %psum.47 = f32[128,64]{0,1:T(8,128)} all-reduce(f32[128,64]{0,1:T(8,128)S(1)} %broadcast_multiply_fusion.1), channel_id=1, replica_groups=mesh['head'=16,'key'=8,'row'=2] {'head','key'}, use_global_device_ids=true, to_apply=%region_15.16 | all-reduce | flops 8192 | bytes 65536 | tf_op jit(solution)/shard_map/psum | solution.py:57
  1243.5 0.0 all-reduce.6.cloned.1.call-done
  1243.5 1.0 constant_dynamic-slice_fusion
  1244.4 0.9 copy.24
  1245.3 0.0 reduce-scatter.2.cloned.1.call-done
  (2 shorter events, 0.0 us)
Async XLA Ops:
  7.2 15.6 %copy-start = (bf16[128,8,576]{0,2,1:T(8,128)(2,1)S(1)}, bf16[128,8,576]{0,2,1:T(8,128)(2,1)}, u32[]{:S(2)}) copy-start(bf16[128,8,576]{0,2,1:T(8,128)(2,1)} %param.5) | copy-start | bytes 3538948
  7.2 529.8 %all-reduce.4.cloned.1.call-start = ((), (), s32[]{:S(2)}) async-start(), calls=%async_computation.1 | async-start | bytes 4194304 | tf_op jit(solution)/shard_map/psum | solution.py:26
  22.7 31.0 %copy-start.1 = (bf16[128,64,128]{2,1,0:T(8,128)(2,1)S(1)}, bf16[128,64,128]{2,1,0:T(8,128)(2,1)}, u32[]{:S(2)}) copy-start(bf16[128,64,128]{2,1,0:T(8,128)(2,1)} %param.7) | copy-start | bytes 6291460
  22.7 31.0 %copy-start.3 = (bf16[256,128]{1,0:T(8,128)(2,1)S(1)}, bf16[256,128]{1,0:T(8,128)(2,1)}, u32[]{:S(2)}) copy-start(bf16[256,128]{1,0:T(8,128)(2,1)} %param.8) | copy-start | bytes 196612
  22.7 31.0 %copy-start.4 = (f32[128,64]{0,1:T(8,128)S(1)}, f32[128,64]{0,1:T(8,128)}, u32[]{:S(2)}) copy-start(f32[128,64]{0,1:T(8,128)} %param.9) | copy-start | bytes 98308
  443.7 799.8 %all-reduce.6.cloned.1.call-start = ((), (), s32[]{:S(2)}) async-start(), calls=%async_computation.2 | async-start | bytes 8388608 | tf_op jit(solution)/shard_map/psum | solution.py:57
  543.8 4.8 copy-start.2
  543.8 4.8 copy-start.5
  543.8 701.5 %reduce-scatter.2.cloned.1.call-start = ((), (), s32[]{:S(2)}) async-start(), calls=%async_computation.3 | async-start | bytes 196608 | tf_op jit(solution)/shard_map/reduce_scatter | solution.py:55
Sparse Core Ops, SparseCore 0:
  443.8 93.1 all-reduce.3
  543.9 234.7 all-reduce.5
  781.8 9.8 reduce-scatter.1

commit v2 on v0

--- a/solution.py
+++ b/solution.py
@@ -54,7 +54,7 @@
     )
     key_grad = lax.psum_scatter(keys_part, "row", scatter_dimension=0, tiled=True)
     head_share = query_part.shape[1] // head_count
-    query_full, weight_grad = lax.psum((query_part, weight_part), ("head", "key"))
+    query_full, weight_grad = lax.psum(lax.psum((query_part, weight_part), "head"), "key")
     query_grad = lax.dynamic_slice_in_dim(
         query_full, lax.axis_index("head") * head_share, head_share, 1
     )

time: 1500 us -> 1040 us (0.69)
  blocking collectives: 1410 us -> 827 us
  waiting for transfers between devices: 0.05 us -> 116 us
    psum x1 -> x2, blocking collectives: 684 us -> 103 us  [the longest x1 72.4 us: shards(): lax.psum((query_part, weight_part), 'head')]
    psum x1 -> x2, waiting for transfers between devices: 0.01 us -> 106 us  [the longest x1 106 us: shards(): lax.psum((query_part, weight_part), 'head')]
  transfers between devices with their start and end apart: 3 -> 4, of which waited for: 0 -> 2; matrix products, arithmetic and copies ran while one was open for 1% -> 2% of each run, Pallas kernels for 0% -> 0%
where the time goes in v2:
time: 1040 us; the launch traced here: 1030 us
  blocking collectives  827 us (80%)
  waiting for transfers between devices  116 us (11%)
  matrix products  32.1 us (3%)
  other arithmetic  22.6 us (2%)
  local copies, waits for them, and re-layouts  22.2 us (2%)
  between operations  13.9 us (1%)
    pmax x1, blocking collectives, shards(): top_logit = lax.pmax(jnp.max(logits, axis=1), ('head', 'key'))  349 us
    psum x1, blocking collectives, shards(): logit_sum = lax.psum(jnp.sum(exp_logit, axis=1), ('head', 'key'))  342 us
    psum x1, waiting for transfers between devices, shards(): lax.psum((query_part, weight_part), 'head')  106 us
    psum x1, blocking collectives, shards(): lax.psum((query_part, weight_part), 'head')  72.4 us
    psum x1, blocking collectives, shards(): lax.psum(lax.psum((query_part, weight_part), 'head'), 'key')  31 us
  transfers between devices with their start and end apart: 4, of which 2 were waited for; matrix products, arithmetic and copies ran while one was open for 2% of the time, Pallas kernels for 0%

profile of v2, /device:TPU:0, one launch (start us, length us, event | category | flops | bytes accessed | tf_op | source)
XLA Modules:
  0.0 1034.1 jit_solution(6784016708318351702)
XLA Ops:
  7.2 0.0 copy-start
  7.2 0.0 all-reduce.4.cloned.1.call-start
  7.2 7.2 copy.19
  14.4 8.3 reshape.73
  22.7 0.0 copy-done
  22.7 12.6 %multiply_reduce_fusion.1 = (f32[128,8]{0,1:T(8,128)S(1)}, f32[128,8,4096]{2,0,1:T(8,128)}) fusion(bf16[128,8,576]{0,2,1:T(8,128)(2,1)S(1)} %copy-done, bf16[4096,576,1]{0,1,2:T(8,128)(2,1)} %reshape.73), kind=kOutput, calls=%fused_computation.2 | convolution fusion | flops 4840225792 | bytes 22679552 | tf_op jit(solution)/shard_map/thd,sd->ths/dot_general | solution.py:17
  35.3 18.2 %pmax.15 = f32[128,8]{0,1:T(8,128)S(1)} all-reduce(f32[128,8]{0,1:T(8,128)S(1)} %get-tuple-element.12), channel_id=1, replica_groups=mesh['head'=16,'key'=8,'row'=2] {'key'}, use_global_device_ids=true, to_apply=%region_6.0 | all-reduce | flops 1024 | bytes 8192 | tf_op jit(solution)/shard_map/pmax | solution.py:20
  53.6 8.6 fusion
  62.2 14.2 %psum.50 = f32[128,8]{0,1:T(8,128)S(1)} all-reduce(f32[128,8]{0,1:T(8,128)S(1)} %fusion), channel_id=1, replica_groups=mesh['head'=16,'key'=8,'row'=2] {'key'}, use_global_device_ids=true, to_apply=%region_8.0 | all-reduce | flops 1024 | bytes 8192 | tf_op jit(solution)/shard_map/psum | solution.py:22
  76.4 8.0 multiply_reduce_fusion
  84.4 0.0 copy-start.2
  84.4 0.0 copy-start.3
  84.4 0.2 broadcast_multiply_fusion
  84.6 1.9 copy.20
  86.4 3.0 copy.21
  89.4 0.0 all-reduce.4.cloned.1.call-update
  89.4 0.2 all-reduce.6.cloned.1.call-start
  89.7 0.0 copy-done.2
  89.7 0.0 copy-done.3
  89.7 6.8 multiply_reduce_fusion.3
  96.4 0.1 multiply_reduce_fusion.4
  96.5 349.1 %pmax.14 = f32[128]{0:T(128)S(1)} all-reduce(f32[128]{0:T(128)S(1)} %multiply_reduce_fusion.4), channel_id=1, replica_groups=mesh['head'=16,'key'=8,'row'=2] {'head','key'}, use_global_device_ids=true, to_apply=%region_2.0 | all-reduce | flops 128 | bytes 1024 | tf_op jit(solution)/shard_map/pmax | solution.py:36
  445.7 0.2 exponential_reduce_fusion
  445.9 342.2 %psum.49 = f32[128]{0:T(128)S(1)} all-reduce(f32[128]{0:T(128)S(1)} %exponential_reduce_fusion), channel_id=1, replica_groups=mesh['head'=16,'key'=8,'row'=2] {'head','key'}, use_global_device_ids=true, to_apply=%region_4.0 | all-reduce | flops 128 | bytes 1024 | tf_op jit(solution)/shard_map/psum | solution.py:38
  788.0 0.0 all-reduce.4.cloned.1.call-done
  788.0 1.0 fusion.12
  789.1 5.7 fusion.13
  794.8 0.0 copy-start.1
  794.8 0.0 all-reduce.6.cloned.1.call-update
  794.8 0.0 all-reduce.8.cloned.1.call-start
  794.9 106.4 %all-reduce.6.cloned.1.call-done = f32[128,64,128]{2,0,1:T(8,128)} async-done(((f32[128,64,128]{2,0,1:T(8,128)}), f32[128,64,128]{2,0,1:T(8,128)}) %all-reduce.6.cloned.1.call-update) | async-done | bytes 4194320 | tf_op jit(solution)/shard_map/psum | solution.py:57
  901.3 0.0 all-reduce.8.cloned.1.call-update
  901.3 0.0 reduce-scatter.2.cloned.1.call-start
  901.3 4.5 multiply_reduce_fusion.2
  905.9 0.0 copy-done.1
  905.9 7.0 fusion.5
  912.9 0.0 reduce-scatter.2.cloned.1.call-update
  913.0 72.4 %psum.54 = f32[128,64]{0,1:T(8,128)S(1)} all-reduce(f32[128,64]{0,1:T(8,128)S(1)} %broadcast_multiply_fusion.1), channel_id=1, replica_groups=mesh['head'=16,'key'=8,'row'=2] {'head'}, use_global_device_ids=true, to_apply=%region_15.16 | all-reduce | flops 8192 | bytes 65536 | tf_op jit(solution)/shard_map/psum | solution.py:57
  985.3 31.0 %psum.55 = f32[128,64]{0,1:T(8,128)} all-reduce(f32[128,64]{0,1:T(8,128)S(1)} %psum.54), channel_id=1, replica_groups=mesh['head'=16,'key'=8,'row'=2] {'key'}, use_global_device_ids=true, to_apply=%region_16.17 | all-reduce | flops 8192 | bytes 65536 | tf_op jit(solution)/shard_map/psum | solution.py:57
  1016.3 0.0 all-reduce.8.cloned.1.call-done
  1016.3 1.0 constant_dynamic-slice_fusion
  1017.3 0.9 copy.24
  1018.1 9.5 reduce-scatter.2.cloned.1.call-done
  (2 shorter events, 0.0 us)
Async XLA Ops:
  7.2 15.6 %copy-start = (bf16[128,8,576]{0,2,1:T(8,128)(2,1)S(1)}, bf16[128,8,576]{0,2,1:T(8,128)(2,1)}, u32[]{:S(2)}) copy-start(bf16[128,8,576]{0,2,1:T(8,128)(2,1)} %param.5) | copy-start | bytes 3538948
  7.2 780.8 %all-reduce.4.cloned.1.call-start = ((), (), s32[]{:S(2)}) async-start(), calls=%async_computation.1 | async-start | bytes 4194304 | tf_op jit(solution)/shard_map/psum | solution.py:26
  84.4 5.3 copy-start.2
  84.4 5.3 copy-start.3
  89.4 811.8 %all-reduce.6.cloned.1.call-start = ((), (), s32[]{:S(2)}) async-start(), calls=%async_computation.2 | async-start | bytes 8388608 | tf_op jit(solution)/shard_map/psum | solution.py:57
  794.8 111.1 %copy-start.1 = (bf16[128,64,128]{2,1,0:T(8,128)(2,1)S(1)}, bf16[128,64,128]{2,1,0:T(8,128)(2,1)}, u32[]{:S(2)}) copy-start(bf16[128,64,128]{2,1,0:T(8,128)(2,1)} %param.7) | copy-start | bytes 6291460
  794.8 221.5 %all-reduce.8.cloned.1.call-start = ((), (), s32[]{:S(2)}) async-start(), calls=%async_computation.3 | async-start | bytes 8388608 | tf_op jit(solution)/shard_map/psum | solution.py:57
  901.3 126.3 %reduce-scatter.2.cloned.1.call-start = ((), (), s32[]{:S(2)}) async-start(), calls=%async_computation.4 | async-start | bytes 196608 | tf_op jit(solution)/shard_map/reduce_scatter | solution.py:55
Sparse Core Ops, SparseCore 0:
  89.5 99.6 all-reduce.3
  795.0 106.2 all-reduce.5
  903.8 109.4 all-reduce.7
  1016.3 11.2 reduce-scatter.1
